TPU v7x, 512 devices: a whole 4x4x16 slice. The times are simulated.
512 devices in a mesh: row: 32 (over z_lo, x), col: 16 (over y, z_hi, core).
Axes of the slice: x: 4, y: 4, z: 16 (z_hi: 2, z_lo: 8; z = z_hi * 8 + z_lo), core: 2. Of those that a mesh axis runs over, the one named last changes fastest.
Arguments:
- anchors: float32 [4096, 4096], P(('row', 'col')), may hold values from 0.2 to 5
- destinations: float32 [4096, 4096], P(('row', 'col')), may hold values from 0.2 to 5
- dest_balance: float32 [4096, 4096], P(('row', 'col')), may hold values from 0.5 to 2
- kernel_hat: float32 [2, 8192, 8192], P(None, ('row', 'col')), as said below
Outputs:
- anchor_balance: float32 [4096, 4096], P(('row', 'col'))
- dest_balance_new: float32 [4096, 4096], P(('row', 'col'))
Inputs may be any that keep to these rules, and one draw needn't show every extreme that they name: kernel_hat[0, b, a] and kernel_hat[1, b, a] are the real and imaginary parts of F(kernel)[a, b] for a table kernel of 8192 x 8192 entries, indexed by a row offset and a column offset taken modulo 8192, that is zero on row 4096 and on column 4096 and positive everywhere else.
All inputs are finite; a program needn't handle non-finite values.
Results may differ from a plain program's by a relative error of at most 0.000072.
Values sent between devices are 32-bit elements; how exact they have to be, the bound alone decides.
A program may use at most 64 MiB of HBM per device.

v0:
```python
import functools

import jax
import jax.numpy as jnp
import ml_dtypes
import numpy as np
from jax import lax
from jax.experimental import pallas as pl
from jax.experimental.pallas import tpu as pltpu
from jax.sharding import PartitionSpec as P

MESH = pl.DeviceIdType.MESH
F32 = jnp.float32
BF16 = jnp.bfloat16
PAD = 8192
FAR_FIRST = [8] + [v for j in range(7, 0, -1) for v in (j, -j)] + [0]


def slot_devices():
    slot = np.arange(512)
    z, p = slot // 32, slot % 32
    return ((z % 8) * 4 + p // 8) * 16 + ((p % 8) // 2) * 4 + (z // 8) * 2 + p % 2


def phase(left, right, modulus):
    return np.exp(-2j * np.pi * (np.outer(left, right) % modulus) / modulus)


def halves(table):
    table = np.asarray(table, np.float32)
    high = table.astype(ml_dtypes.bfloat16)
    return high, (table - high.astype(np.float32)).astype(ml_dtypes.bfloat16)


def lanes_matrix(small):
    real, imag = small.real, small.imag
    block = np.stack([np.stack([real, imag], 1), np.stack([-imag, real], 1)], 0)
    out = np.zeros((2, 8, 8, 2, 8, 8))
    for freq in range(8):
        out[:, :, freq, :, :, freq] = block
    return out.reshape(128, 128)


def turn_pair(table):
    count = table.shape[0]
    real = np.broadcast_to(table.real, (count, 8, 8)).reshape(count, 64)
    imag = np.broadcast_to(table.imag, (count, 8, 8)).reshape(count, 64)
    t1 = np.concatenate([real, real], 1)
    t2 = np.concatenate([-imag, imag], 1)
    return t1.astype(np.float32), t2.astype(np.float32)


def make_tables():
    dev = slot_devices()
    fine = np.arange(512)
    eight = np.arange(8)
    sets = (eight, eight + 1)
    out = {}
    first = np.zeros((128, 256))
    last = np.zeros((256, 128))
    for half in range(2):
        form = np.zeros((8, 8, 2, 8, 8))
        turn = phase(eight, sets[half], 16)
        for s in range(8):
            form[:, s, 0, s, :] = turn.real
            form[:, s, 1, s, :] = turn.imag
        form = form.reshape(64, 128)
        first[:64, half * 128 : half * 128 + 128] = form
        last[half * 128 : half * 128 + 128, :64] = 2.0 * form.T / (PAD * PAD)
    out["first"] = halves(first)
    out["last"] = halves(last)
    pairs = [turn_pair(phase(fine, sets[half], PAD)[:, None, :]) for half in range(2)]
    out["rowturn"] = [np.concatenate([pairs[0][i], pairs[1][i]], 1) for i in range(2)]
    rows = phase(dev, fine, 512)
    out["rowfwd"] = halves(np.concatenate([rows.real, rows.imag], 1))
    back = rows.conj().T
    out["rowinv"] = halves(
        np.concatenate(
            [
                part[:, block * 128 : block * 128 + 128]
                for block in range(4)
                for part in (back.real, back.imag)
            ],
            1,
        )
    )
    cols = phase(np.arange(1024), dev, 1024)
    out["colfwd"] = halves(np.concatenate([cols.real, cols.imag], 1))
    back = cols.conj().T
    out["colinv"] = halves(
        np.concatenate(
            [
                part[:, block * 512 : block * 512 + 512]
                for block in range(2)
                for part in (back.real, back.imag)
            ],
            1,
        )
    )
    out["colturn"] = turn_pair(phase(np.arange(1024), eight, PAD)[:, :, None])
    for name, mat in (("eightf", phase(eight, eight, 8)), ("eighti", phase(eight, eight, 8).conj())):
        out[name] = halves(lanes_matrix(mat))
    return out


ORDER = ("first", "rowturn", "rowfwd", "colfwd", "colturn", "eightf", "eighti", "colinv", "rowinv", "last")


def split(x):
    high = x.astype(BF16)
    return high, (x - high.astype(F32)).astype(BF16)


def dot(a, b):
    return jnp.dot(a, b, preferred_element_type=F32)


def lane_dot(x, high, low):
    xh, xl = split(x)
    return dot(xh, high) + dot(xl, high) + dot(xh, low)


def swap(x):
    return pltpu.roll(x, 64, 1)


def kernel(anchors, dest, bal, khat, *refs):
    hbm = refs[:20]
    ab_out, db_out = refs[20:22]
    (vanch, vdest, vbal, vk, k4, *vt) = refs[22 : 22 + 5 + 20]
    (ka, kb, kc, sent, got, zb, gz, lsem, ssem, rsem, ksem, all_in) = refs[47:]
    tab = {name: (vt[2 * i], vt[2 * i + 1]) for i, name in enumerate(ORDER)}

    row, col = lax.axis_index("row"), lax.axis_index("col")
    z = (col // 2 % 2) * 8 + row // 4
    p = (row % 4) * 8 + (col // 4) * 2 + col % 2
    me = z * 32 + p

    def device(zz, pp):
        return ((zz % 8) * 4 + pp // 8, ((pp % 8) // 2) * 4 + (zz // 8) * 2 + pp % 2)

    loads = {}

    def load(name, src, dst):
        copy = pltpu.make_async_copy(src, dst, lsem.at[len(loads)])
        loads[name] = copy
        copy.start()

    load("dest", dest, vdest)
    load("bal", bal, vbal)
    for i in range(3 * 2):
        load((ORDER[i // 2], i % 2), hbm[i], vt[i])
    load("khat", khat, vk)
    for i in range(3 * 2, 20):
        load((ORDER[i // 2], i % 2), hbm[i], vt[i])
    load("anchors", anchors, vanch)

    k4[...] = jnp.zeros_like(k4)
    barrier = pltpu.get_barrier_semaphore()

    def greet_z(k, carry):
        pl.semaphore_signal(barrier, inc=1, device_id=device((z + k) % 16, p), device_id_type=MESH)
        return carry

    def greet_p(k, carry):
        pl.semaphore_signal(barrier, inc=1, device_id=device(z, (p + k) % 32), device_id_type=MESH)
        return carry

    lax.fori_loop(1, 16, greet_z, 0)
    lax.fori_loop(1, 32, greet_p, 0)

    lane = lax.broadcasted_iota(jnp.int32, (1, 128), 1)
    freq0 = lane % 8 == 0
    re_lane = lane < 64
    re0 = (freq0 & re_lane).astype(F32)
    im0 = (freq0 & (lane >= 64)).astype(F32)
    alt = 1.0 - 2.0 * (lax.broadcasted_iota(jnp.int32, (512, 128), 0) % 2).astype(F32)
    neg_re = jnp.where(re_lane, -1.0, 1.0).astype(F32)

    def stack_turned(x):
        return jnp.concatenate([x, swap(x) * neg_re], 0)

    def table_dot(refs_, rows, cols, x):
        xh, xl = split(x)
        wide = dot(refs_[0][rows, cols], jnp.concatenate([xh, xl], 1))
        return wide[:, :128] + wide[:, 128:] + dot(refs_[1][rows, cols], xh)

    def rows_forward(v, out):
        blocks = [v[:, 512 * i : 512 * i + 512] for i in range(8)]
        v64 = jnp.concatenate(blocks + [jnp.zeros((64, 512), F32)], 0)
        vt_ = v64.T
        h = lane_dot(vt_, tab["first"][0][...], tab["first"][1][...])
        hs = []
        for half in range(2):
            lanes = slice(half * 128, half * 128 + 128)
            g = h[:, lanes]
            hs.append(g * tab["rowturn"][0][:, lanes] + swap(g) * tab["rowturn"][1][:, lanes])
        nyq = swap(jnp.sum(hs[0] * alt, axis=0, keepdims=True)) * im0
        for half in range(2):
            x = stack_turned(hs[half])
            for part in range(2):
                rows = slice((2 * part + half) * 128, (2 * part + half) * 128 + 128)
                out[rows, :] = table_dot(tab["rowfwd"], rows, slice(None), x)
        out[0:1, :] = out[0:1, :] + nyq

    def rows_inverse(src):
        acc = jnp.zeros((512, 128), F32)
        top = src[0:1, :]
        nyq = swap(top * im0) * 0.5
        for half in range(2):
            g = jnp.zeros((512, 128), F32)
            for part in range(2):
                block = 2 * part + half
                x = src[block * 128 : block * 128 + 128, :]
                if block == 0:
                    keep = 1.0 - 0.5 * re0 - im0
                    first_row = lax.broadcasted_iota(jnp.int32, (128, 128), 0) == 0
                    x = jnp.where(first_row, x * keep, x)
                g = g + table_dot(
                    tab["rowinv"], slice(None), slice(block * 256, block * 256 + 256), stack_turned(x)
                )
            if half == 0:
                g = g + alt * nyq
            lanes = slice(half * 128, half * 128 + 128)
            g = g * tab["rowturn"][0][:, lanes] - swap(g) * tab["rowturn"][1][:, lanes]
            acc = acc + lane_dot(g, tab["last"][0][lanes, :], tab["last"][1][lanes, :])
        y64 = acc.T
        return jnp.concatenate([y64[8 * i : 8 * i + 8, :] for i in range(8)], 1)

    def columns(src, out, turn):
        zb[0] = stack_turned(src[...])

        @pl.when(me == 0)
        def _():
            zb[1] = stack_turned(src[...] * (-neg_re))

        for chunk in range(2):
            rows = slice(chunk * 512, chunk * 512 + 512)
            t1, t2 = tab["colturn"][0][rows, :], tab["colturn"][1][rows, :]

            def spectrum(which):
                g = table_dot(tab["colfwd"], rows, slice(None), zb[which])
                g = g * t1 + swap(g) * t2
                return lane_dot(g, tab["eightf"][0][...], tab["eightf"][1][...])

            y = spectrum(0)
            gz[...] = y * ka[rows, :] + swap(y) * (turn * kb[rows, :])

            @pl.when(me == 0)
            def _():
                yc = spectrum(1)
                kct = kc[rows, :]
                kcs = swap(kct)
                kca = jnp.where(re_lane, kct, kcs)
                kcb = jnp.where(re_lane, -kcs, kct)
                gz[...] = gz[...] + yc * kca + swap(yc) * (turn * kcb)

            g = lane_dot(gz[...], tab["eighti"][0][...], tab["eighti"][1][...])
            g = g * t1 - swap(g) * t2
            part = table_dot(
                tab["colinv"], slice(None), slice(chunk * 1024, chunk * 1024 + 1024), stack_turned(g)
            )
            out[...] = part if chunk == 0 else out[...] + part

    def exchange(step):
        src, dst = sent.at[step], got.at[step]
        for offset in FAR_FIRST:
            zz = (z + offset + 16) % 16

            def send(k, carry):
                pp = (p + k) % 32
                pltpu.make_async_remote_copy(
                    src_ref=src.at[pl.ds(zz * 32 + pp, 1)],
                    dst_ref=dst.at[pl.ds(me, 1)],
                    send_sem=ssem.at[step],
                    recv_sem=rsem.at[step],
                    device_id=device(zz, pp),
                    device_id_type=MESH,
                ).start()
                return carry

            lax.fori_loop(1 if offset == 0 else 0, 32, send, 0, unroll=1 if offset == 0 else 8)
        own = pltpu.make_async_copy(src.at[pl.ds(me, 1)], dst.at[pl.ds(me, 1)], lsem.at[24])
        own.start()
        own.wait()
        everything = pltpu.make_async_remote_copy(
            src_ref=src.at[pl.ds(0, 511)],
            dst_ref=dst.at[pl.ds(0, 511)],
            send_sem=ssem.at[step],
            recv_sem=rsem.at[step],
            device_id=device(z, p),
            device_id_type=MESH,
        )
        everything.wait_send()
        everything.wait_recv()

    for key in ("dest", "bal") + tuple((n, i) for n in ORDER[:3] for i in range(2)):
        loads.pop(key).wait()
    rows_forward(vbal[...] * vdest[...], sent.at[0])

    pl.semaphore_wait(barrier, 46)

    def tell_z(k, carry):
        pl.semaphore_signal(all_in, inc=1, device_id=device((z + k) % 16, p), device_id_type=MESH)
        return carry

    lax.fori_loop(1, 16, tell_z, 0)
    pl.semaphore_wait(all_in, 15)

    exchange_k4(row, col, vk, k4, ksem, loads)
    for key in tuple(loads):
        loads.pop(key).wait()
    exchange(0)

    low = row < 16
    pieces = []
    for c in range(2):
        for m in range(8):
            lanes = slice(m * 1024, m * 1024 + 1024)
            pieces.append(jnp.where(low, vk[c, 0:8, lanes], vk[c, 1:9, lanes]))
    kt = jnp.concatenate(pieces, 0).T
    ks = swap(kt)
    ka[...] = jnp.where(re_lane, kt, ks)
    kb[...] = jnp.where(re_lane, -ks, kt)

    @pl.when(me == 0)
    def _():
        wait_k4(vk, k4, ksem)
        own = jnp.where(re_lane, ka[...], kb[...])
        nyq_pieces = []
        for c in range(2):
            for m in range(8):
                nyq_pieces.append(k4[c, :, m * 1024 : m * 1024 + 1024])
        nyq = jnp.concatenate(nyq_pieces, 0).T
        kc[...] = jnp.where(freq0, 0.5 * (own - nyq), 0.0)
        mean = jnp.where(freq0, 0.5 * (own + nyq), own)
        ms = swap(mean)
        ka[...] = jnp.where(re_lane, mean, ms)
        kb[...] = jnp.where(re_lane, -ms, mean)

    columns(got.at[0], sent.at[1], -1.0)
    exchange(1)
    ab = 1.0 / rows_inverse(got.at[1])
    ab_out[...] = ab
    rows_forward(ab * vanch[...], sent.at[2])
    exchange(2)
    columns(got.at[2], sent.at[3], 1.0)
    exchange(3)
    db_out[...] = 1.0 / rows_inverse(got.at[3])


def k4_copy(vk, k4, ksem, device_id):
    return pltpu.make_async_remote_copy(
        src_ref=vk.at[:, pl.ds(0, 1)],
        dst_ref=k4.at[:, pl.ds(0, 1)],
        send_sem=ksem.at[0],
        recv_sem=ksem.at[1],
        device_id=device_id,
        device_id_type=MESH,
    )


def exchange_k4(row, col, vk, k4, ksem, loads):
    loads.pop("khat").wait()

    @pl.when((row == 16) & (col == 0))
    def _():
        copy = k4_copy(vk, k4, ksem, (row - 16, col))
        copy.start()
        copy.wait_send()


def wait_k4(vk, k4, ksem):
    row, col = lax.axis_index("row"), lax.axis_index("col")
    k4_copy(vk, k4, ksem, (row + 16, col)).wait_recv()


def per_device(anchors, destinations, dest_balance, kernel_hat):
    tables = make_tables()
    consts = [jnp.asarray(t) for name in ORDER for t in tables[name]]
    vmem = pl.BlockSpec(memory_space=pltpu.VMEM)
    anywhere = pl.BlockSpec(memory_space=pl.ANY)
    grid = jax.ShapeDtypeStruct(anchors.shape, F32)
    dma = pltpu.SemaphoreType.DMA
    scratch = [pltpu.VMEM(anchors.shape, F32)] * 3
    scratch += [pltpu.VMEM(kernel_hat.shape, F32), pltpu.VMEM((2, 8, PAD), F32)]
    scratch += [pltpu.VMEM(c.shape, c.dtype) for c in consts]
    scratch += [pltpu.VMEM((1024, 128), F32)] * 3
    scratch += [pltpu.VMEM((4, 512, 128), F32)] * 2
    scratch += [pltpu.VMEM((2, 1024, 128), F32), pltpu.VMEM((512, 128), F32)]
    scratch += [dma((32,)), dma((4,)), dma((4,)), dma((2,)), pltpu.SemaphoreType.REGULAR]
    return pl.pallas_call(
        kernel,
        out_shape=(grid, grid),
        in_specs=[anywhere] * (4 + len(consts)),
        out_specs=(vmem, vmem),
        scratch_shapes=scratch,
        compiler_params=pltpu.CompilerParams(
            collective_id=0, has_side_effects=True, vmem_limit_bytes=56 << 20
        ),
        cost_estimate=pl.CostEstimate(flops=4 << 30, bytes_accessed=20 << 20, transcendentals=0),
    )(anchors, destinations, dest_balance, kernel_hat, *consts)


def solution(mesh):
    rows = P(("row", "col"), None)
    return jax.shard_map(
        per_device,
        mesh=mesh,
        in_specs=(rows, rows, rows, P(None, ("row", "col"), None)),
        out_specs=(rows, rows),
        check_vma=False,
    )
```

profile of v0, /device:TPU:1, one launch (start us, length us, event | category | flops | bytes accessed | tf_op | source)
XLA Modules:
  0.0 109.7 jit_solution(11991582560339092368)
XLA Ops:
  0.6 106.0 %shard_map.239 = (f32[8,4096]{1,0:T(8,128)}, f32[8,4096]{1,0:T(8,128)}) custom-call(f32[8,4096]{1,0:T(8,128)} %anchors.1, f32[8,4096]{1,0:T(8,128)} %dest.1, f32[8,4096]{1,0:T(8,128)} %bal.1, f32[2,16,8192]{2,1,0:T(8,128)} %khat.1, bf16[128,256]{1,0:T(8,128)(2,1)} %constant.40.clone.refs_0_, bf16[128,256]{1,0:T(8,128)(2,1)} %constant.41.clone.refs_1_, ...), custom_call_target="tpu_custom_call" | custom-call | flops 4294967296 | bytes 20971520 | tf_op jit(solution)/shard_map/pallas_call | solution.py:392
  106.6 1.6 %copy.28 = f32[8,4096]{1,0:T(8,128)} copy(f32[8,4096]{1,0:T(8,128)} %get-tuple-element.4) | data formatting | bytes 262144
  108.2 1.6 %copy.29 = f32[8,4096]{1,0:T(8,128)} copy(f32[8,4096]{1,0:T(8,128)} %get-tuple-element.5) | data formatting | bytes 262144
where the time goes:
time: 110 us
  Pallas kernels  106 us (96%)
  local copies, waits for them, and re-layouts  3.14 us (3%)
    pallas_call x1, Pallas kernels, per_device(): pl.pallas_call(kernel, out_shape=(grid, grid), in_specs=[anywhere] * (4 +...  106 us
    unnamed x2, local copies, waits for them, and re-layouts  3.14 us

commit v1 on v0

v1 whole, which is shorter than its diff:
```python
import functools

import jax
import jax.numpy as jnp
import ml_dtypes
import numpy as np
from jax import lax
from jax.experimental import pallas as pl
from jax.experimental.pallas import tpu as pltpu
from jax.sharding import PartitionSpec as P

MESH = pl.DeviceIdType.MESH
F32 = jnp.float32
BF16 = jnp.bfloat16
PAD = 8192
TRANSLATIONS = [(i, j, k) for i in (2, 1, 3, 0) for j in (2, 1, 3, 0) for k in (1, 0)]


def slot_devices():
    slot = np.arange(512)
    z, p = slot // 32, slot % 32
    return ((z % 8) * 4 + p // 8) * 16 + ((p % 8) // 2) * 4 + (z // 8) * 2 + p % 2


def phase(left, right, modulus):
    return np.exp(-2j * np.pi * (np.outer(left, right) % modulus) / modulus)


def halves(table):
    table = np.asarray(table, np.float32)
    high = table.astype(ml_dtypes.bfloat16)
    return high, (table - high.astype(np.float32)).astype(ml_dtypes.bfloat16)


def stacked(table):
    high, low = halves(table)
    return np.concatenate([high, high], 0), low


def lanes_matrix(small):
    real, imag = small.real, small.imag
    block = np.stack([np.stack([real, imag], 1), np.stack([-imag, real], 1)], 0)
    out = np.zeros((2, 8, 8, 2, 8, 8))
    for freq in range(8):
        out[:, :, freq, :, :, freq] = block
    return out.reshape(128, 128)


def turn_pair(table):
    count = table.shape[0]
    real = np.broadcast_to(table.real, (count, 8, 8)).reshape(count, 64)
    imag = np.broadcast_to(table.imag, (count, 8, 8)).reshape(count, 64)
    t1 = np.concatenate([real, real], 1)
    t2 = np.concatenate([-imag, imag], 1)
    return t1.astype(np.float32), t2.astype(np.float32)


def make_tables():
    dev = slot_devices()
    fine = np.arange(512)
    eight = np.arange(8)
    sets = (eight, eight + 1)
    out = {}
    first = np.zeros((128, 256))
    last = np.zeros((256, 128))
    for half in range(2):
        form = np.zeros((8, 8, 2, 8, 8))
        turn = phase(eight, sets[half], 16)
        for s in range(8):
            form[:, s, 0, s, :] = turn.real
            form[:, s, 1, s, :] = turn.imag
        form = form.reshape(64, 128)
        first[:64, half * 128 : half * 128 + 128] = form
        last[half * 128 : half * 128 + 128, :64] = 2.0 * form.T / (PAD * PAD)
    out["first"] = stacked(first)
    out["last"] = tuple(
        np.concatenate(pair, 0) for pair in zip(stacked(last[:128]), stacked(last[128:]))
    )
    pairs = [turn_pair(phase(fine, sets[half], PAD)[:, None, :]) for half in range(2)]
    out["rowturn"] = [np.concatenate([pairs[0][i], pairs[1][i]], 1) for i in range(2)]
    even = np.concatenate([np.arange(128), np.arange(256, 384)])
    rows = phase(np.concatenate([dev[even], dev[even + 128]]), fine, 512)
    out["rowfwd"] = halves(np.concatenate([rows.real, rows.imag], 1))
    back = phase(fine, dev, 512).conj()
    out["rowinv"] = halves(
        np.concatenate(
            [
                part[:, block * 128 : block * 128 + 128]
                for block in range(4)
                for part in (back.real, back.imag)
            ],
            1,
        )
    )
    base = dev[even]
    quarter = np.arange(256)
    cols = phase(quarter, base, 256)
    out["colfwd"] = halves(np.concatenate([cols.real, cols.imag], 1))
    back = cols.conj().T
    out["colinv"] = halves(np.concatenate([back.real, back.imag], 1))
    turns = np.concatenate([phase(base, np.array([r]), 1024) for r in range(1, 4)], 0)
    out["devturn"] = turn_pair(turns[:, :, None])
    freqs = (quarter[None, :] * 4 + np.arange(4)[:, None]).reshape(-1)
    out["colturn"] = turn_pair(phase(freqs, eight, PAD)[:, :, None])
    packed = np.where(eight < 4, phase(freqs, eight, PAD).reshape(4, 256, 8, 1)[eight % 4, :, :, 0].transpose(1, 2, 0), 0.0)
    out["packturn"] = turn_pair(packed)
    for name, mat in (("eightf", phase(eight, eight, 8)), ("eighti", phase(eight, eight, 8).conj())):
        out[name] = stacked(lanes_matrix(mat))
    return out


ORDER = (
    "first", "rowturn", "rowfwd", "devturn", "colfwd", "colturn", "packturn", "eightf", "eighti", "colinv", "rowinv", "last",
)
TABLES = 2 * len(ORDER)


def split(x):
    high = x.astype(BF16)
    return high, (x - high.astype(F32)).astype(BF16)


def dot(a, b):
    return jnp.dot(a, b, preferred_element_type=F32)


def lane_dot(x, high, low):
    xh, xl = split(x)
    return dot(jnp.concatenate([xh, xl], 1), high) + dot(xh, low)


def swap(x):
    return pltpu.roll(x, 64, 1)


def kernel(anchors, dest, bal, khat, *refs):
    hbm, refs = refs[:TABLES], refs[TABLES:]
    (factors, vanch, vdest, vbal, vk, k4), refs = refs[:6], refs[6:]
    vt, refs = refs[:TABLES], refs[TABLES:]
    (kt, ka, kb, kc, sent, got, gz, lsem, ssem, rsem, ksem, all_in) = refs
    tab = {name: (vt[2 * i], vt[2 * i + 1]) for i, name in enumerate(ORDER)}

    row, col = lax.axis_index("row"), lax.axis_index("col")
    z = (col // 2 % 2) * 8 + row // 4
    p = (row % 4) * 8 + (col // 4) * 2 + col % 2
    me = z * 32 + p

    xs = [lax.rem(row + i, 4) for i in range(4)]
    ys = [lax.rem(lax.div(col, 4) + i, 4) for i in range(4)]
    cores = [lax.rem(col, 2), 1 - lax.rem(col, 2)]

    def z_base(zz):
        return lax.rem(zz, 8) * 4, lax.div(zz, 8) * 2

    def z_device(offset):
        first_row, first_col = z_base(lax.rem(z + offset, 16))
        return first_row + xs[0], first_col + (ys[0] * 4 + cores[0])

    loads = {}

    def load(name, src, dst):
        copy = pltpu.make_async_copy(src, dst, lsem.at[len(loads)])
        loads[name] = copy
        copy.start()

    load("dest", dest, vdest)
    load("bal", bal, vbal)
    for i in range(3 * 2):
        load((ORDER[i // 2], i % 2), hbm[i], vt[i])
    k4[...] = jnp.zeros_like(k4)
    barrier = pltpu.get_barrier_semaphore()

    for offset in range(1, 16):
        pl.semaphore_signal(barrier, inc=1, device_id=z_device(offset), device_id_type=MESH)
    own_row, own_col = z_base(z)
    for i, j, k in TRANSLATIONS[:-1]:
        target = (own_row + xs[i], own_col + (ys[j] * 4 + cores[k]))
        pl.semaphore_signal(barrier, inc=1, device_id=target, device_id_type=MESH)

    load("khat", khat, vk)
    for i in range(3 * 2, TABLES):
        load((ORDER[i // 2], i % 2), hbm[i], vt[i])
    load("anchors", anchors, vanch)

    lane = lax.broadcasted_iota(jnp.int32, (1, 128), 1)
    freq0 = lane % 8 == 0
    re_lane = lane < 64
    re0 = (freq0 & re_lane).astype(F32)
    im0 = (freq0 & (lane >= 64)).astype(F32)
    alt = 1.0 - 2.0 * (lax.broadcasted_iota(jnp.int32, (512, 128), 0) % 2).astype(F32)
    neg_re = jnp.where(re_lane, -1.0, 1.0).astype(F32)

    def times_i(x):
        return swap(x) * neg_re

    def stack_turned(x):
        return jnp.concatenate([x, times_i(x)], 0)

    def table_dot(refs_, rows, cols, x):
        xh, xl = split(x)
        wide = dot(refs_[0][rows, cols], jnp.concatenate([xh, xl], 1))
        return wide[:, :128] + wide[:, 128:] + dot(refs_[1][rows, cols], xh)

    def rows_forward(v, out):
        blocks = [v[:, 512 * i : 512 * i + 512] for i in range(8)]
        v64 = jnp.concatenate(blocks + [jnp.zeros((64, 512), F32)], 0)
        vt_ = v64.T
        h = lane_dot(vt_, tab["first"][0][...], tab["first"][1][...])
        hs = []
        for half in range(2):
            lanes = slice(half * 128, half * 128 + 128)
            g = h[:, lanes]
            hs.append(g * tab["rowturn"][0][:, lanes] + swap(g) * tab["rowturn"][1][:, lanes])
        nyq = swap(jnp.sum(hs[0] * alt, axis=0, keepdims=True)) * im0
        for half in range(2):
            x = stack_turned(hs[half])
            y = table_dot(tab["rowfwd"], slice(256 * half, 256 * half + 256), slice(None), x)
            out[128 * half : 128 * half + 128, :] = y[:128]
            out[128 * half + 256 : 128 * half + 384, :] = y[128:]
        out[0:1, :] = out[0:1, :] + nyq

    def rows_inverse(src):
        acc = jnp.zeros((512, 128), F32)
        top = src[0:1, :]
        nyq = swap(top * im0) * 0.5
        for half in range(2):
            g = jnp.zeros((512, 128), F32)
            for part in range(2):
                block = 2 * part + half
                x = src[block * 128 : block * 128 + 128, :]
                if block == 0:
                    keep = 1.0 - 0.5 * re0 - im0
                    first_row = lax.broadcasted_iota(jnp.int32, (128, 128), 0) == 0
                    x = jnp.where(first_row, x * keep, x)
                g = g + table_dot(
                    tab["rowinv"], slice(None), slice(block * 256, block * 256 + 256), stack_turned(x)
                )
            if half == 0:
                g = g + alt * nyq
            lanes = slice(half * 128, half * 128 + 128)
            g = g * tab["rowturn"][0][:, lanes] - swap(g) * tab["rowturn"][1][:, lanes]
            acc = acc + lane_dot(
                g, tab["last"][0][256 * half : 256 * half + 256, :], tab["last"][1][lanes, :]
            )
        y64 = acc.T
        return jnp.concatenate([y64[8 * i : 8 * i + 8, :] for i in range(8)], 1)

    def dev_turn(x, r, sign):
        rows = slice(256 * r - 256, 256 * r)
        return x * tab["devturn"][0][rows, :] + swap(x) * (sign * tab["devturn"][1][rows, :])

    def pack(parts):
        kept = [jnp.where(freq0, part, 0.0) for part in parts]
        return kept[0] + pltpu.roll(kept[1], 1, 1) + pltpu.roll(kept[2], 2, 1) + pltpu.roll(kept[3], 3, 1)

    def columns(src, out, turn):
        def folded(r, flip):
            a = jnp.concatenate([src[0:128, :], src[256:384, :]], 0) * flip
            b = jnp.concatenate([src[128:256, :], src[384:512, :]], 0) * flip
            if r % 2:
                b = times_i(b)
            u = a + b if r in (0, 3) else a - b
            return dev_turn(u, r, 1.0) if r else u

        def spectrum(u, turns, rows):
            g = table_dot(tab["colfwd"], slice(None), slice(None), stack_turned(u))
            g = g * turns[0][rows, :] + swap(g) * turns[1][rows, :]
            return lane_dot(g, tab["eightf"][0][...], tab["eightf"][1][...])

        for r in range(4):
            rows = slice(256 * r, 256 * r + 256)
            y = spectrum(folded(r, 1.0), tab["colturn"], rows)
            gz[rows, :] = y * ka[rows, :] + swap(y) * (turn * kb[rows, :])

        @pl.when(me == 0)
        def _():
            u = pack([folded(r, -neg_re) for r in range(4)])
            yc = spectrum(u, tab["packturn"], slice(None))
            kct = kc[...]
            kcs = swap(kct)
            kca = jnp.where(re_lane, kct, kcs)
            kcb = jnp.where(re_lane, -kcs, kct)
            more = yc * kca + swap(yc) * (turn * kcb)
            for r in range(4):
                rows = slice(256 * r, 256 * r + 256)
                part = pltpu.roll(more, 128 - r, 1) if r else more
                gz[rows, :] = gz[rows, :] + jnp.where(freq0, part, 0.0)

        upper, lower = [], []
        for r in range(4):
            rows = slice(256 * r, 256 * r + 256)
            g = lane_dot(gz[rows, :], tab["eighti"][0][...], tab["eighti"][1][...])
            g = g * tab["colturn"][0][rows, :] - swap(g) * tab["colturn"][1][rows, :]
            v = table_dot(tab["colinv"], slice(None), slice(None), stack_turned(g))
            if r:
                v = dev_turn(v, r, -1.0)
            upper.append(v)
            lower.append(times_i(v) if r % 2 else v)
        first = (upper[0] + upper[2]) + (upper[1] + upper[3])
        second = (lower[0] - lower[2]) + (lower[1] - lower[3])
        out[0:128, :] = first[:128]
        out[128:256, :] = second[:128]
        out[256:384, :] = first[128:]
        out[384:512, :] = second[128:]

    def send_group(step, zz, moves):
        first_row, first_col = z_base(zz)
        first_slot = zz * 32
        for i, j, k in moves:
            slot = first_slot + (xs[i] * 8 + ys[j] * 2 + cores[k])
            pltpu.make_async_remote_copy(
                src_ref=sent.at[step, pl.ds(slot, 1)],
                dst_ref=got.at[step, pl.ds(me, 1)],
                send_sem=ssem.at[step],
                recv_sem=rsem.at[step],
                device_id=(first_row + xs[i], first_col + (ys[j] * 4 + cores[k])),
                device_id_type=MESH,
            ).start()

    def send_plane(step):
        send_group(step, z, TRANSLATIONS[:-1])

    def send_far(step):
        def one(i, carry):
            distance = 8 - (i + 1) // 2
            offset = jnp.where(i % 2 == 1, distance, 16 - distance)
            send_group(step, lax.rem(z + offset, 16), TRANSLATIONS)
            return carry

        lax.fori_loop(0, 15, one, 0)

    def exchange_wait(step):
        src, dst = sent.at[step], got.at[step]
        own = pltpu.make_async_copy(src.at[pl.ds(me, 1)], dst.at[pl.ds(me, 1)], lsem.at[31])
        own.start()
        own.wait()
        everything = pltpu.make_async_remote_copy(
            src_ref=src.at[pl.ds(0, 511)],
            dst_ref=dst.at[pl.ds(0, 511)],
            send_sem=ssem.at[step],
            recv_sem=rsem.at[step],
            device_id=z_device(0),
            device_id_type=MESH,
        )
        everything.wait_send()
        everything.wait_recv()

    for key in ("dest", "bal") + tuple((n, i) for n in ORDER[:3] for i in range(2)):
        loads.pop(key).wait()
    rows_forward(vbal[...] * vdest[...], sent.at[0])

    pl.semaphore_wait(barrier, 46)

    for offset in range(1, 16):
        pl.semaphore_signal(all_in, inc=1, device_id=z_device(offset), device_id_type=MESH)

    exchange_k4(row, col, vk, k4, ksem, loads)
    send_plane(0)
    pl.semaphore_wait(all_in, 15)

    low = row < 16

    def own_piece(c, lanes):
        return jnp.where(low, vk[c, 0:8, lanes], vk[c, 1:9, lanes])

    def nyq_piece(c, lanes):
        return k4[c, :, lanes]

    def turn_rows(piece, j):
        lanes = [slice(m * 1024 + j * 128, m * 1024 + j * 128 + 128) for m in range(8)]
        kt[128 * j : 128 * j + 128, :] = jnp.concatenate(
            [piece(c, lanes[m]) for c in range(2) for m in range(8)], 0
        ).T

    def residue(r):
        return kt[pl.ds(r, 256, stride=4), :]

    def store_spectrum(r, spec):
        rows = slice(256 * r, 256 * r + 256)
        turned = swap(spec)
        ka[rows, :] = jnp.where(re_lane, spec, turned)
        kb[rows, :] = jnp.where(re_lane, -turned, spec)

    steps = [functools.partial(turn_rows, own_piece, j) for j in range(8)]
    steps += [lambda r=r: store_spectrum(r, residue(r)) for r in range(4)]

    def finish_loads():
        for key in tuple(loads):
            loads.pop(key).wait()

    send_far(0)
    for piece in steps + [finish_loads]:
        piece()

    @pl.when(me == 0)
    def _():
        wait_k4(vk, k4, ksem)
        for j in range(8):
            turn_rows(nyq_piece, j)
        apart = []
        for r in range(4):
            rows = slice(256 * r, 256 * r + 256)
            own = jnp.where(re_lane, ka[rows, :], kb[rows, :])
            nyq = residue(r)
            apart.append(0.5 * (own - nyq))
            store_spectrum(r, jnp.where(freq0, 0.5 * (own + nyq), own))
        kc[...] = pack(apart)

    exchange_wait(0)
    columns(got.at[0], sent.at[1], -1.0)
    send_far(1)
    send_plane(1)
    exchange_wait(1)
    ab = 1.0 / rows_inverse(got.at[1])
    factors[0:8, :] = ab
    rows_forward(ab * vanch[...], sent.at[2])
    send_far(2)
    send_plane(2)
    exchange_wait(2)
    columns(got.at[2], sent.at[3], 1.0)
    send_far(3)
    send_plane(3)
    exchange_wait(3)
    factors[8:16, :] = 1.0 / rows_inverse(got.at[3])


def k4_copy(vk, k4, ksem, device_id):
    return pltpu.make_async_remote_copy(
        src_ref=vk.at[:, pl.ds(0, 1)],
        dst_ref=k4.at[:, pl.ds(0, 1)],
        send_sem=ksem.at[0],
        recv_sem=ksem.at[1],
        device_id=device_id,
        device_id_type=MESH,
    )


def exchange_k4(row, col, vk, k4, ksem, loads):
    loads.pop("khat").wait()

    @pl.when((row == 16) & (col == 0))
    def _():
        copy = k4_copy(vk, k4, ksem, (row - 16, col))
        copy.start()
        copy.wait_send()


def wait_k4(vk, k4, ksem):
    row, col = lax.axis_index("row"), lax.axis_index("col")
    k4_copy(vk, k4, ksem, (row + 16, col)).wait_recv()


def per_device(anchors, destinations, dest_balance, kernel_hat):
    tables = make_tables()
    consts = [jnp.asarray(t) for name in ORDER for t in tables[name]]
    vmem = pl.BlockSpec(memory_space=pltpu.VMEM)
    anywhere = pl.BlockSpec(memory_space=pl.ANY)
    count, width = anchors.shape
    dma = pltpu.SemaphoreType.DMA
    scratch = [pltpu.VMEM(anchors.shape, F32)] * 3
    scratch += [pltpu.VMEM(kernel_hat.shape, F32), pltpu.VMEM((2, 8, PAD), F32)]
    scratch += [pltpu.VMEM(c.shape, c.dtype) for c in consts]
    scratch += [pltpu.VMEM((1024, 128), F32)] * 3 + [pltpu.VMEM((256, 128), F32)]
    scratch += [pltpu.VMEM((4, 512, 128), F32)] * 2
    scratch += [pltpu.VMEM((1024, 128), F32)]
    scratch += [dma((32,)), dma((4,)), dma((4,)), dma((2,)), pltpu.SemaphoreType.REGULAR]
    factors = pl.pallas_call(
        kernel,
        out_shape=jax.ShapeDtypeStruct((2 * count, width), F32),
        in_specs=[anywhere] * (4 + len(consts)),
        out_specs=vmem,
        scratch_shapes=scratch,
        compiler_params=pltpu.CompilerParams(
            collective_id=0, has_side_effects=True, vmem_limit_bytes=56 << 20
        ),
        cost_estimate=pl.CostEstimate(flops=4 << 30, bytes_accessed=20 << 20, transcendentals=0),
    )(anchors, destinations, dest_balance, kernel_hat, *consts)
    return factors[:count], factors[count:]


def solution(mesh):
    rows = P(("row", "col"), None)
    return jax.shard_map(
        per_device,
        mesh=mesh,
        in_specs=(rows, rows, rows, P(None, ("row", "col"), None)),
        out_specs=(rows, rows),
        check_vma=False,
    )
```

time: 110 us -> 102 us (0.927)
  Pallas kernels: 106 us -> 99.5 us
  local copies, waits for them, and re-layouts: 3.14 us -> 1.69 us
    pallas_call x1, Pallas kernels: 106 us -> 99.5 us  [per_device(): pl.pallas_call(kernel, out_shape=jax.ShapeDtypeStruct((2 * count, width),...]
    unnamed x2 -> x0, local copies, waits for them, and re-layouts: 3.14 us -> none
    slice x0 -> x1, local copies, waits for them, and re-layouts: none -> 1.69 us  [per_device(): return (factors[:count], factors[count:])]
where the time goes in v1:
time: 102 us
  Pallas kernels  99.5 us (98%)
  local copies, waits for them, and re-layouts  1.69 us (2%)
    pallas_call x1, Pallas kernels, per_device(): pl.pallas_call(kernel, out_shape=jax.ShapeDtypeStruct((2 * count, width),...  99.5 us

profile of v1, /device:TPU:1, one launch (start us, length us, event | category | flops | bytes accessed | tf_op | source)
XLA Modules:
  0.0 101.8 jit_solution(8103856070475061099)
XLA Ops:
  0.6 99.5 %shard_map.275 = f32[16,4096]{1,0:T(8,128)} custom-call(f32[8,4096]{1,0:T(8,128)} %anchors.1, f32[8,4096]{1,0:T(8,128)} %dest.1, f32[8,4096]{1,0:T(8,128)} %bal.1, f32[2,16,8192]{2,1,0:T(8,128)} %khat.1, bf16[256,256]{1,0:T(8,128)(2,1)} %constant.48.clone.refs_0_, bf16[128,256]{1,0:T(8,128)(2,1)} %constant.49.clone.refs_1_, ...), custom_call_target="tpu_custom_call" | custom-call | flops 4294967296 | bytes 20971520 | tf_op jit(solution)/shard_map/pallas_call | solution.py:467
  100.1 1.7 %fusion = (f32[8,4096]{1,0:T(8,128)}, f32[8,4096]{1,0:T(8,128)}) fusion(f32[16,4096]{1,0:T(8,128)} %shard_map.275), kind=kLoop, calls=%fused_computation | loop fusion | bytes 524288 | tf_op jit(solution)/shard_map/slice | solution.py:478
